TPU v7x, 32 devices: a whole 2x2x4 slice. The times are simulated.
32 devices in a mesh: section: 8 (over z, y), dp: 4 (over x, core).
Axes of the slice: x: 2, y: 2, z: 4, core: 2. Of those that a mesh axis runs over, the one named last changes fastest.
Arguments:
- initial_block_entries: bfloat16 [4, 8, 144, 5120], P('dp', 'section'), may hold values from -6 to 6
- incoming_tokens: bfloat16 [4, 3, 128, 5120], P('dp', None, None, 'section'), may hold values from -6 to 6
- adjoint_flow: bfloat16 [4, 8, 4, 144, 5120], P('dp', 'section'), may hold values from -6 to 6
- address_projector: bfloat16 [8, 5120, 128], P('section', 'dp'), may hold values from -0.078125 to 0.078125
- rescale_factor: bfloat16 [8, 5120], P('section'), may hold values from 0.5 to 1.5
- storage_rate_projector: bfloat16 [8, 5120], P('section'), may hold values from -0.078125 to 0.078125
- associative_store: float32 [4, 8, 128, 5120], P('dp', 'section'), may hold values from -480 to 480
- recall_scaling: float32 [4, 8, 128], P('dp', 'section'), may hold values from 4 to 40
Outputs:
- final_tick_outcomes: bfloat16 [4, 8, 144, 5120], P('dp', 'section')
- address_derivative: float32 [8, 5120, 128], P('section', 'dp')
All inputs are finite; a program needn't handle non-finite values.
Results may differ from a plain program's by a relative error of at most 0.0061.
Values may be sent and summed in bfloat16 or wider, within the bound.
A program may use at most 128 MiB of HBM per device.

v0:
```python
import jax
import jax.numpy as jnp
from jax import lax
from jax.sharding import PartitionSpec as P

HIGH = lax.Precision.HIGHEST


def from_behind(array, axis, by):
    peers = lax.axis_size(axis)
    return lax.ppermute(array, axis, [(i, (i + by) % peers) for i in range(peers)])


def per_device(
    initial_block_entries,
    incoming_tokens,
    adjoint_flow,
    address_projector,
    rescale_factor,
    storage_rate_projector,
    associative_store,
    recall_scaling,
):
    leading_block = lax.axis_index("section") == 0
    seg_rows = incoming_tokens.shape[2]
    ticks = adjoint_flow.shape[2]
    line_breadth = initial_block_entries.shape[3]
    keysize = address_projector.shape[2]
    gain_row = rescale_factor[0].astype(jnp.float32)
    beta_col = storage_rate_projector[0]
    value_rows = associative_store[0, 0]
    norm_values = recall_scaling[0, 0]
    whole = lax.all_gather(address_projector[0], "dp", axis=0, tiled=True)
    recurrent_vector = initial_block_entries[0, 0]
    produced_entries = recurrent_vector
    local_total = jnp.zeros((line_breadth, keysize), jnp.float32)
    for tick in range(ticks):
        if tick > 0:
            columns = lax.all_gather(incoming_tokens[0, tick - 1], "section", axis=1, tiled=True)
            shifted_along = from_behind(produced_entries, "section", 1)
            loop_rows = shifted_along[seg_rows:]
            attention_channel = jnp.concatenate([columns, loop_rows], axis=0)
            recurrent_vector = jnp.where(leading_block, attention_channel, shifted_along)
        channel_features = recurrent_vector.astype(jnp.float32)
        meansq = jnp.mean(channel_features * channel_features, axis=-1, keepdims=True)
        normed = (channel_features * lax.rsqrt(meansq + 1e-06) * gain_row).astype(jnp.bfloat16)
        pre = jnp.dot(normed, whole, preferred_element_type=jnp.float32)
        query = jax.nn.elu(pre) + 1.0
        num = jnp.dot(query, value_rows, precision=HIGH)
        den = 1.0 + jnp.dot(query, norm_values, precision=HIGH)
        produced_entries = (channel_features + num / den[:, None]).astype(jnp.bfloat16)
        grad_out = adjoint_flow[0, 0, tick].astype(jnp.float32)
        dnum = grad_out / den[:, None]
        dden = -jnp.sum(grad_out * num, axis=-1) / (den * den)
        dq = (
            jnp.einsum("rd,kd->rk", dnum, value_rows, precision=HIGH)
            + dden[:, None] * norm_values[None, :]
        )
        slope = jnp.where(pre > 0, 1.0, jnp.exp(jnp.minimum(pre, 0.0)))
        key_cot = (dq * slope).astype(jnp.bfloat16)
        term = jnp.einsum("rd,rk->dk", normed, key_cot, preferred_element_type=jnp.float32)
        local_total = local_total + term
        mem_keys = query[seg_rows:]
        mem_vals = normed[seg_rows:].astype(jnp.float32)
        beta = jax.nn.sigmoid(
            jnp.dot(normed[seg_rows:], beta_col, preferred_element_type=jnp.float32)
        )
        prev = jnp.dot(mem_keys, value_rows, precision=HIGH)
        prev = prev / (1.0 + jnp.dot(mem_keys, norm_values, precision=HIGH))[:, None]
        value_rows = value_rows + jnp.einsum(
            "rk,rd->kd", mem_keys, beta[:, None] * (mem_vals - prev), precision=HIGH
        )
        norm_values = norm_values + jnp.einsum("rk,r->k", mem_keys, beta, precision=HIGH)
    summed = lax.psum_scatter(local_total, "dp", scatter_dimension=0, tiled=True)
    return (produced_entries[None, None], summed[None])


def solution(mesh):
    placed = (
        P("dp", "section", None, None),
        P("dp", None, None, "section"),
        P("dp", "section", None, None, None),
        P("section", "dp", None),
        P("section", None),
        P("section", None),
        P("dp", "section", None, None),
        P("dp", "section", None),
    )
    return jax.shard_map(
        per_device,
        mesh=mesh,
        in_specs=placed,
        out_specs=(P("dp", "section", None, None), P("section", "dp", None)),
        check_vma=False,
    )
```

profile of v0, /device:TPU:0, one launch (start us, length us, event | category | flops | bytes accessed | tf_op | source)
XLA Modules:
  0.0 277.7 jit_solution(6938049443331020091)
XLA Ops:
  7.2 0.7 all-gather.15.cloned.1.call-update
  8.0 1.9 fusion.160
  9.9 1.8 fusion.29
  11.7 0.4 fusion.31
  12.2 18.3 %all-gather.15.cloned.1.call-done = bf16[1,5120,128]{2,1,0:T(8,128)(2,1)} async-done(((bf16[1,1280,128]{2,1,0:T(8,128)(2,1)}), bf16[1,5120,128]{2,1,0:T(8,128)(2,1)}) %all-gather.15.cloned.1.call-update) | async-done | bytes 1310736 | tf_op jit(solution)/shard_map/all_gather | solution.py:33
  30.5 2.0 fusion.99
  32.8 5.0 %fusion.32 = (bf16[144,5120]{1,0:T(8,128)(2,1)}, f32[144,5120]{1,0:T(8,128)}) fusion(bf16[1,1,144,5120]{3,2,1,0:T(8,128)(2,1)S(1)} %copy-done.16, f32[144]{0:T(256)S(1)} %broadcast_add_fusion.3, f32[1,1,128,5120]{3,2,1,0:T(8,128)S(1)} %copy-done.12, f32[144,128]{1,0:T(8,128)S(1)} %get-tuple-element.17), kind=kOutput, calls=%fused_computation.60 | convolution fusion | flops 1135484928 | bytes 8593984 | tf_op jit(solution)/shard_map/dot_general | solution.py:49
  37.8 1.5 collective-permute-start
  39.3 0.6 all-gather.9.cloned.1.call-start
  40.4 3.4 %fusion.5 = f32[16,5120]{1,0:T(8,128)S(1)} fusion(f32[1,1,128,5120]{3,2,1,0:T(8,128)} %param.14, f32[16]{0:T(128)S(1)} %fusion.80, f32[16]{0:T(128)S(1)} %fusion.92, bf16[144,5120]{1,0:T(8,128)(2,1)S(1)} %fusion.31, f32[144,128]{1,0:T(8,128)S(1)} %get-tuple-element.16), kind=kOutput, calls=%fused_computation.14 | convolution fusion | flops 126156800 | bytes 3122176 | tf_op jit(solution)/shard_map/dot_general | solution.py:68
  43.8 3.8 %convolution_add_fusion.2 = f32[128,5120]{1,0:T(8,128)} fusion(f32[16,5120]{1,0:T(8,128)S(1)} %fusion.5, f32[1,1,128,5120]{3,2,1,0:T(8,128)S(1)} %copy-done.13, f32[144,128]{1,0:T(8,128)S(1)} %get-tuple-element.16), kind=kOutput, calls=%fused_computation.2 | convolution fusion | flops 126484480 | bytes 5578752 | tf_op jit(solution)/shard_map/rk,rd->kd/dot_general | solution.py:70
  47.7 43.4 %collective-permute-done = bf16[144,5120]{1,0:T(8,128)(2,1)S(1)} collective-permute-done((bf16[144,5120]{1,0:T(8,128)(2,1)}, bf16[144,5120]{1,0:T(8,128)(2,1)S(1)}, u32[]{:S(2)}, u32[]{:S(2)}) %collective-permute-start) | collective-permute-done | bytes 1474592 | tf_op jit(solution)/shard_map/ppermute | solution.py:11
  91.1 2.1 fusion.17
  93.2 0.4 fusion.19
  93.7 0.6 fusion.101
  94.2 0.2 fusion.145
  94.5 0.5 copy-done.2
  94.9 5.0 %fusion.20 = (bf16[144,5120]{1,0:T(8,128)(2,1)}, f32[144,5120]{1,0:T(8,128)}) fusion(bf16[144,5120]{1,0:T(8,128)(2,1)S(1)} %get-tuple-element.11, f32[144]{0:T(256)S(1)} %broadcast_add_fusion.2, f32[128,5120]{1,0:T(8,128)S(1)} %copy-done.2, f32[144,128]{1,0:T(8,128)S(1)} %get-tuple-element.21), kind=kOutput, calls=%fused_computation.48 | convolution fusion | flops 1135484928 | bytes 8593984 | tf_op jit(solution)/shard_map/dot_general | solution.py:49
  100.0 0.2 reduce-scatter.2.cloned.1.call-start
  100.6 3.3 %fusion.3 = f32[16,5120]{1,0:T(8,128)S(1)} fusion(f32[128,5120]{1,0:T(8,128)} %convolution_add_fusion.2, f32[16]{0:T(128)S(1)} %fusion.78, f32[16]{0:T(128)S(1)} %fusion.88, bf16[144,5120]{1,0:T(8,128)(2,1)S(1)} %fusion.19, f32[144,128]{1,0:T(8,128)S(1)} %get-tuple-element.20), kind=kOutput, calls=%fused_computation.11 | convolution fusion | flops 126156800 | bytes 3122176 | tf_op jit(solution)/shard_map/dot_general | solution.py:68
  104.0 3.9 %convolution_add_fusion.1 = f32[128,5120]{1,0:T(8,128)} fusion(f32[128,5120]{1,0:T(8,128)S(1)} %copy-done.3, f32[16,5120]{1,0:T(8,128)S(1)} %fusion.3, f32[144,128]{1,0:T(8,128)S(1)} %get-tuple-element.20), kind=kOutput, calls=%fused_computation.1 | convolution fusion | flops 126484480 | bytes 5578752 | tf_op jit(solution)/shard_map/rk,rd->kd/dot_general | solution.py:70
  107.9 42.7 %collective-permute-done.1 = bf16[144,5120]{1,0:T(8,128)(2,1)} collective-permute-done((bf16[144,5120]{1,0:T(8,128)(2,1)}, bf16[144,5120]{1,0:T(8,128)(2,1)}, u32[]{:S(2)}, u32[]{:S(2)}) %collective-permute-start.1) | collective-permute-done | bytes 1474592 | tf_op jit(solution)/shard_map/ppermute | solution.py:11
  150.6 0.9 slice.70
  151.6 2.1 fusion.21
  153.7 0.4 fusion.23
  154.2 0.5 fusion.105
  154.7 0.2 fusion.141
  154.9 1.0 copy-done.5
  156.0 4.5 %fusion.24 = (bf16[144,5120]{1,0:T(8,128)(2,1)S(1)}, f32[144,5120]{1,0:T(8,128)}) fusion(bf16[144,5120]{1,0:T(8,128)(2,1)S(1)} %get-tuple-element.9, f32[144]{0:T(256)S(1)} %broadcast_add_fusion.1, f32[128,5120]{1,0:T(8,128)S(1)} %copy-done.5, f32[144,128]{1,0:T(8,128)S(1)} %get-tuple-element.25), kind=kOutput, calls=%fused_computation.52 | convolution fusion | flops 1135484928 | bytes 8593984 | tf_op jit(solution)/shard_map/dot_general | solution.py:49
  161.2 1.4 fusion.1
  162.5 3.8 %convolution_add_fusion = f32[128,5120]{1,0:T(8,128)} fusion(f32[128,5120]{1,0:T(8,128)S(1)} %copy-done.5, f32[16,5120]{1,0:T(8,128)S(1)} %fusion.1, f32[144,128]{1,0:T(8,128)S(1)} %get-tuple-element.24), kind=kOutput, calls=%fused_computation | convolution fusion | flops 126484480 | bytes 5578752 | tf_op jit(solution)/shard_map/rk,rd->kd/dot_general | solution.py:70
  166.3 42.0 %collective-permute-done.2 = bf16[144,5120]{1,0:T(8,128)(2,1)S(1)} collective-permute-done((bf16[144,5120]{1,0:T(8,128)(2,1)S(1)}, bf16[144,5120]{1,0:T(8,128)(2,1)S(1)}, u32[]{:S(2)}, u32[]{:S(2)}) %collective-permute-start.2) | collective-permute-done | bytes 1474592 | tf_op jit(solution)/shard_map/ppermute | solution.py:11
  208.3 1.1 copy-done.20
  209.5 2.2 fusion.25
  211.7 0.7 fusion.45
  212.6 0.8 copy-done.15
  213.4 2.6 fusion.114
  216.1 5.0 %fusion.16 = (f32[144]{0:T(256)S(1)}, f32[144]{0:T(256)S(1)}, f32[144]{0:T(256)S(1)}, f32[144]{0:T(256)S(1)}, bf16[1,1,144,5120]{3,2,1,0:T(8,128)(2,1)}) fusion(f32[144,5120]{1,0:T(8,128)S(1)} %fusion.114, bf16[1,1,4,144,5120]{4,3,2,1,0:T(8,128)(2,1)} %param.10, f32[144,5120]{1,0:T(8,128)S(1)} %copy-done.17, f32[144,5120]{1,0:T(8,128)S(1)} %copy-done.18, ...), kind=kLoop, calls=%fused_computation.44 | loop fusion | flops 11795904 | bytes 20646720 | tf_op jit(solution)/shard_map/reduce_sum | solution.py:54
  221.1 2.8 fusion.107
  223.9 2.8 fusion.111
  226.7 2.8 fusion.103
  229.5 2.8 fusion.70
  232.3 1.3 fusion.161
  233.5 1.0 convolution_add_fusion.5
  234.5 0.4 copy-done.8
  234.9 0.9 convolution_add_fusion.4
  235.9 2.6 convolution_add_fusion.3
  238.4 32.4 %reduce-scatter.2.cloned.1.call-done = f32[1280,128]{1,0:T(8,128)} async-done(((f32[5120,128]{1,0:T(8,128)}), f32[1280,128]{1,0:T(8,128)}) %reduce-scatter.2.cloned.1.call-update) | async-done | bytes 655376 | tf_op jit(solution)/shard_map/reduce_scatter | solution.py:74
  (82 shorter events, 2.4 us)
Async XLA Ops:
  7.2 32.8 %copy-start = (bf16[1,5120]{1,0:T(2,128)(2,1)S(1)}, bf16[1,5120]{1,0:T(2,128)(2,1)}, u32[]{:S(2)}) copy-start(bf16[1,5120]{1,0:T(2,128)(2,1)} %param.13) | copy-start | bytes 30724
  7.2 4.5 %copy-start.16 = (bf16[1,1,144,5120]{3,2,1,0:T(8,128)(2,1)S(1)}, bf16[1,1,144,5120]{3,2,1,0:T(8,128)(2,1)}, u32[]{:S(2)}) copy-start(bf16[1,1,144,5120]{3,2,1,0:T(8,128)(2,1)} %param.8) | copy-start | bytes 4423684
  7.2 4.5 %copy-start.21 = (bf16[1,5120]{1,0:T(2,128)(2,1)S(1)}, bf16[1,5120]{1,0:T(2,128)(2,1)}, u32[]{:S(2)}) copy-start(bf16[1,5120]{1,0:T(2,128)(2,1)} %param.12) | copy-start | bytes 30724
  7.2 23.3 %all-gather.15.cloned.1.call-start = ((), (), s32[]{:S(2)}) async-start(), calls=%async_computation.5 | async-start | bytes 1638400 | tf_op jit(solution)/shard_map/all_gather | solution.py:33
  7.9 83.1 %all-gather.13.cloned.1.call-start = ((), (), s32[]{:S(2)}) async-start(), calls=%async_computation.4 | async-start | bytes 1474560 | tf_op jit(solution)/shard_map/all_gather | solution.py:39
  9.9 141.7 %all-gather.11.cloned.1.call-start = ((), (), s32[]{:S(2)}) async-start(), calls=%async_computation.3 | async-start | bytes 1474560 | tf_op jit(solution)/shard_map/all_gather | solution.py:39
  11.7 20.8 %copy-start.22 = (f32[1,1,128]{2,1,0:T(1,128)S(1)}, f32[1,1,128]{2,1,0:T(1,128)}, u32[]{:S(2)}) copy-start(f32[1,1,128]{2,1,0:T(1,128)} %param.15) | copy-start | bytes 1540
  30.5 2.3 copy-start.12
  37.8 53.2 %collective-permute-start = (bf16[144,5120]{1,0:T(8,128)(2,1)}, bf16[144,5120]{1,0:T(8,128)(2,1)S(1)}, u32[]{:S(2)}, u32[]{:S(2)}) collective-permute-start(bf16[144,5120]{1,0:T(8,128)(2,1)} %get-tuple-element.18), channel_id=1, source_target_pairs={{0,4},{4,8},{8,12},{12,16},{16,20},{20,24},{24,28},{28,0},{1,5},{5... | collective-permute-start | bytes 4423688 | tf_op jit(solution)/shard_map/ppermute | solution.py:11
  39.3 170.1 %all-gather.9.cloned.1.call-start = ((), (), s32[]{:S(2)}) async-start(), calls=%async_computation.2 | async-start | bytes 1474560 | tf_op jit(solution)/shard_map/all_gather | solution.py:39
  40.0 3.9 %copy-start.13 = (f32[1,1,128,5120]{3,2,1,0:T(8,128)S(1)}, f32[1,1,128,5120]{3,2,1,0:T(8,128)}, u32[]{:S(2)}) copy-start(f32[1,1,128,5120]{3,2,1,0:T(8,128)} %param.14) | copy-start | bytes 7864324
  91.1 2.6 copy-start.9
  93.2 1.7 copy-start.2
  99.9 50.7 %collective-permute-start.1 = (bf16[144,5120]{1,0:T(8,128)(2,1)}, bf16[144,5120]{1,0:T(8,128)(2,1)}, u32[]{:S(2)}, u32[]{:S(2)}) collective-permute-start(bf16[144,5120]{1,0:T(8,128)(2,1)} %get-tuple-element.22), channel_id=1, source_target_pairs={{0,4},{4,8},{8,12},{12,16},{16,20},{20,24},{24,28},{28,0},{1,5},{5... | collective-permute-start | bytes 4423688 | tf_op jit(solution)/shard_map/ppermute | solution.py:11
  100.0 170.9 %reduce-scatter.2.cloned.1.call-start = ((), (), s32[]{:S(2)}) async-start(), calls=%async_computation.1 | async-start | bytes 3276800 | tf_op jit(solution)/shard_map/reduce_scatter | solution.py:74
  100.2 3.8 %copy-start.3 = (f32[128,5120]{1,0:T(8,128)S(1)}, f32[128,5120]{1,0:T(8,128)}, u32[]{:S(2)}) copy-start(f32[128,5120]{1,0:T(8,128)} %convolution_add_fusion.2) | copy-start | bytes 7864324
  151.6 2.6 copy-start.10
  153.7 2.3 copy-start.5
  154.2 7.0 %copy-start.7 = (bf16[144,5120]{1,0:T(8,128)(2,1)}, bf16[144,5120]{1,0:T(8,128)(2,1)S(1)}, u32[]{:S(2)}) copy-start(bf16[144,5120]{1,0:T(8,128)(2,1)S(1)} %fusion.23) | copy-start | bytes 4423684
  160.5 47.8 %collective-permute-start.2 = (bf16[144,5120]{1,0:T(8,128)(2,1)S(1)}, bf16[144,5120]{1,0:T(8,128)(2,1)S(1)}, u32[]{:S(2)}, u32[]{:S(2)}) collective-permute-start(bf16[144,5120]{1,0:T(8,128)(2,1)S(1)} %get-tuple-element.26), channel_id=1, source_target_pairs={{0,4},{4,8},{8,12},{12,16},{16,20},{20,24},{24,28},{28,0},{1,5},{5... | collective-permute-start | bytes 4423688 | tf_op jit(solution)/shard_map/ppermute | solution.py:11
  208.3 1.1 copy-start.20
  209.4 2.2 copy-start.11
  209.4 6.6 %copy-start.19 = (f32[144,5120]{1,0:T(8,128)S(1)}, f32[144,5120]{1,0:T(8,128)}, u32[]{:S(2)}) copy-start(f32[144,5120]{1,0:T(8,128)} %get-tuple-element.27) | copy-start | bytes 8847364
  211.6 1.7 copy-start.15
  211.6 4.4 %copy-start.17 = (f32[144,5120]{1,0:T(8,128)S(1)}, f32[144,5120]{1,0:T(8,128)}, u32[]{:S(2)}) copy-start(f32[144,5120]{1,0:T(8,128)} %get-tuple-element.19) | copy-start | bytes 8847364
  211.7 4.4 %copy-start.18 = (f32[144,5120]{1,0:T(8,128)S(1)}, f32[144,5120]{1,0:T(8,128)}, u32[]{:S(2)}) copy-start(f32[144,5120]{1,0:T(8,128)} %get-tuple-element.23) | copy-start | bytes 8847364
  213.4 7.8 %slice-start = ((s8[5898240]{0:T(1024)(128)(4,1)}), s8[4194304]{0:T(1024)(128)(4,1)S(1)}, s32[]{:S(2)}) async-start(s8[5898240]{0:T(1024)(128)(4,1)} %bitcast.210), calls=%async_computation.6 | async-start | bytes 8388608
  216.0 5.1 %copy-start.6 = (f32[128,5120]{1,0:T(8,128)S(1)}, f32[128,5120]{1,0:T(8,128)}, u32[]{:S(2)}) copy-start(f32[128,5120]{1,0:T(8,128)} %convolution_add_fusion.1) | copy-start | bytes 7864324
  216.1 5.1 %slice-start.1 = ((s8[5898240]{0:T(1024)(128)(4,1)}), s8[1703936]{0:T(1024)(128)(4,1)S(1)}, s32[]{:S(2)}) async-start(s8[5898240]{0:T(1024)(128)(4,1)} %bitcast.210), calls=%async_computation.7 | async-start | bytes 3407872
  223.9 2.8 %copy-start.4 = (f32[128,5120]{1,0:T(8,128)S(1)}, f32[128,5120]{1,0:T(8,128)}, u32[]{:S(2)}) copy-start(f32[128,5120]{1,0:T(8,128)} %convolution_add_fusion.2) | copy-start | bytes 7864324
  226.7 2.8 %copy-start.14 = (f32[1,1,128,5120]{3,2,1,0:T(8,128)S(1)}, f32[1,1,128,5120]{3,2,1,0:T(8,128)}, u32[]{:S(2)}) copy-start(f32[1,1,128,5120]{3,2,1,0:T(8,128)} %param.14) | copy-start | bytes 7864324
  233.5 1.4 copy-start.8
  235.9 35.0 %copy-start.1 = (bf16[1,5120]{1,0:T(2,128)(2,1)S(1)}, bf16[1,5120]{1,0:T(2,128)(2,1)}, u32[]{:S(2)}) copy-start(bf16[1,5120]{1,0:T(2,128)(2,1)} %param.13) | copy-start | bytes 30724
Sparse Core Ops, SparseCore 0:
  9.6 20.8 all-gather.14
  32.7 52.8 all-gather.12
  87.9 53.1 all-gather.10
  143.7 52.7 all-gather.8
  238.6 32.2 reduce-scatter.1
where the time goes:
time: 282 us; the launch traced here: 278 us
  waiting for transfers between devices  180 us (64%)
  matrix products  59.5 us (21%)
  between operations  14.6 us (5%)
  other arithmetic  14.5 us (5%)
  local copies, waits for them, and re-layouts  6.78 us (2%)
    ppermute x3, waiting for transfers between devices, from_behind(): lax.ppermute(array, axis, [(i, (i + by) % peers) for i in range(peers)])  128 us
    reduce_scatter x1, waiting for transfers between devices, per_device(): lax.psum_scatter(local_total, 'dp', scatter_dimension=0, tiled=True)  32.4 us
    all_gather x1, waiting for transfers between devices, per_device(): whole = lax.all_gather(address_projector[0], 'dp', axis=0, tiled=True)  18.3 us
    dot_general x4, matrix products, per_device(): num = jnp.dot(query, value_rows, precision=HIGH)  17.1 us
    dot_general x3, matrix products, per_device(): jnp.einsum('rk,rd->kd', mem_keys, beta[:, None] * (mem_vals - prev), prec...  11.5 us
    dot_general x4, matrix products, per_device(): jnp.einsum('rd,kd->rk', dnum, value_rows, precision=HIGH)  11 us
    reduce_sum x4, other arithmetic, per_device(): jnp.mean(channel_features * channel_features, axis=-1, keepdims=True)  8.15 us
    dot_general x3, matrix products, per_device(): prev = jnp.dot(mem_keys, value_rows, precision=HIGH)  8.14 us
  transfers between devices with their start and end apart: 8, of which 5 were waited for; matrix products, arithmetic and copies ran while one was open for 18% of the time, Pallas kernels for 0%

commit v1 on v0

--- a/solution.py
+++ b/solution.py
@@ -1,6 +1,10 @@
+import functools
+
 import jax
 import jax.numpy as jnp
 from jax import lax
+from jax.experimental import pallas as pl
+from jax.experimental.pallas import tpu as pltpu
 from jax.sharding import PartitionSpec as P
 
 HIGH = lax.Precision.HIGHEST
@@ -75,6 +79,342 @@
     return (produced_entries[None, None], summed[None])
 
 
+MESH = pl.DeviceIdType.MESH
+NT = (((1,), (1,)), ((), ()))
+TN = (((0,), (0,)), ((), ()))
+F32 = jnp.float32
+BF16 = jnp.bfloat16
+
+
+def dot(a, b, dims=(((1,), (0,)), ((), ()))):
+    return lax.dot_general(a, b, dims, preferred_element_type=F32)
+
+
+def fused(
+    sections, docs, ticks, seg,
+    h0_any, tok_any, g_any, w_any, gain, rate, a_any, z_in,
+    y_out, ad_out,
+    h0, hbuf, ybuf, g, w_own, w, a32, a16, z, cot, fbuf, kbuf, adt,
+    load_sem, send_w, recv_w, send_tok, recv_tok, send_y, recv_y,
+    send_f, recv_f, send_k, recv_k,
+):
+    sec, me = lax.axis_index("section"), lax.axis_index("dp")
+    rows, width = h0.shape
+    mem = rows - seg
+    span = width // docs
+    cw = width // sections
+    per = span // cw
+    follower = lax.rem(sec + 1, sections)
+    first, last = sec == 0, sec == sections - 1
+
+    def peer(i):
+        return lax.rem(me + i, docs)
+
+    def cols(c, size=cw):
+        return pl.ds(pl.multiple_of(c * size, 128), size)
+
+    def remote(src, dst, send, recv, device):
+        return pltpu.make_async_remote_copy(
+            src_ref=src, dst_ref=dst, send_sem=send, recv_sem=recv,
+            device_id=device, device_id_type=MESH,
+        )
+
+    own_w = w.at[pl.ds(pl.multiple_of(me * span, 128), span)]
+    load_w = pltpu.make_async_copy(w_any.at[0], w_own, load_sem.at[0])
+    load_h = pltpu.make_async_copy(h0_any.at[0, 0], h0, load_sem.at[1])
+    load_a = pltpu.make_async_copy(a_any.at[0, 0], a32, load_sem.at[2])
+    load_g = [
+        pltpu.make_async_copy(g_any.at[0, 0, t], g.at[t], load_sem.at[3 + t])
+        for t in range(ticks)
+    ]
+    load_w.start()
+    load_a.start()
+    load_h.start()
+    for copy in load_g:
+        copy.start()
+
+    barrier = pltpu.get_barrier_semaphore()
+    for i in range(1, docs):
+        pl.semaphore_signal(barrier, inc=1, device_id=(sec, peer(i)), device_id_type=MESH)
+    for i in range(1, sections):
+        pl.semaphore_signal(
+            barrier, inc=1, device_id=(lax.rem(sec + i, sections), me), device_id_type=MESH
+        )
+
+    gain_own = gain[:, cols(me, span)].astype(F32)
+    keys = w.shape[1]
+    gain_col = jnp.broadcast_to(gain_own, (keys, span)).T
+    load_w.wait()
+    own_w[...] = (w_own[...].astype(F32) * gain_col).astype(BF16)
+    pl.semaphore_wait(barrier, docs + sections - 2)
+
+    def w_copy(i):
+        return remote(own_w, own_w, send_w.at[i], recv_w.at[me], (sec, peer(i)))
+
+    def w_wait(i):
+        p = peer(i)
+        block = w.at[pl.ds(pl.multiple_of(p * span, 128), span)]
+        remote(block, block, send_w.at[i], recv_w.at[p], (sec, p)).wait_recv()
+
+    for i in range(1, docs):
+        w_copy(i).start()
+
+    def tok_copy(t):
+        return remote(
+            tok_any.at[0, t], hbuf.at[t, pl.ds(0, seg), cols(sec)],
+            send_tok.at[t], recv_tok.at[t, sec], (0, me),
+        )
+
+    def tok_wait(t, c):
+        dst = hbuf.at[t, pl.ds(0, seg), cols(c)]
+        pltpu.make_async_copy(tok_any.at[0, t], dst, recv_tok.at[t, c]).wait()
+
+    @pl.when(jnp.logical_not(first))
+    def _():
+        for t in range(ticks - 1):
+            tok_copy(t).start()
+
+    @pl.when(first)
+    def _():
+        for t in range(ticks - 1):
+            dst = hbuf.at[t, pl.ds(0, seg), pl.ds(0, cw)]
+            pltpu.make_async_copy(tok_any.at[0, t], dst, recv_tok.at[t, 0]).start()
+
+    def y_whole(t, c):
+        return remote(
+            ybuf.at[t, :, cols(c)], hbuf.at[t, :, cols(c)],
+            send_y.at[t, c], recv_y.at[t, c], (follower, me),
+        )
+
+    def y_mem(t, c):
+        part = pl.ds(seg, mem)
+        return remote(
+            ybuf.at[t, part, cols(c)], hbuf.at[t, part, cols(c)],
+            send_y.at[t, c], recv_y.at[t, c], (follower, me),
+        )
+
+    def forward(t, src, c, owner):
+        dst = fbuf.at[t, me, :, cols(lax.rem(c, per))]
+        return remote(
+            src.at[:, cols(c)], dst, send_f.at[t, c], recv_f.at[t, me, lax.rem(c, per)],
+            (sec, owner),
+        )
+
+    def k_copy(t, i):
+        return remote(
+            kbuf.at[t, me], kbuf.at[t, me], send_k.at[t, i], recv_k.at[t, me], (sec, peer(i))
+        )
+
+    z[...] = z_in[0]
+    load_a.wait()
+    load_g[0].wait()
+
+    def first_cot(c, total):
+        part = a32[:, cols(c)].astype(BF16)
+        a16[:, cols(c)] = part
+        return total + dot(g[0, :, cols(c)], part, NT)
+
+    blank = jnp.zeros((rows, keys), F32)
+    cot[...] = lax.fori_loop(0, sections, first_cot, blank)
+    adt[...] = jnp.zeros_like(adt)
+    load_h.wait()
+    for i in range(1, docs):
+        w_wait(i)
+
+    for t in range(ticks):
+        src = h0 if t == 0 else hbuf.at[t - 1]
+
+        def arrive(c, carry, t=t, src=src):
+            squares, pre = carry
+            if t > 0:
+                @pl.when(first)
+                def _():
+                    tok_wait(t - 1, c)
+                    y_mem(t - 1, c).wait_recv()
+
+                @pl.when(jnp.logical_not(first))
+                def _():
+                    y_whole(t - 1, c).wait_recv()
+
+            owner = lax.div(c, per)
+
+            @pl.when(owner != me)
+            def _():
+                forward(t, src, c, owner).start()
+
+            h = src[:, cols(c)]
+            hf = h.astype(F32)
+            for j in range(cw // 128):
+                piece = hf[:, j * 128:(j + 1) * 128]
+                squares = squares + piece * piece
+            return squares, pre + dot(h, w[cols(c), :])
+
+        squares, pre = lax.fori_loop(
+            0, sections, arrive, (jnp.zeros((rows, 128), F32), blank)
+        )
+        scale = lax.rsqrt(jnp.sum(squares, axis=1, keepdims=True) / width + 1e-06)
+        pre = pre * scale
+        low = jnp.exp(jnp.minimum(pre, 0.0))
+        query = jnp.where(pre > 0, pre + 1.0, low)
+        zrow = z[...]
+        inv = 1.0 / (1.0 + jnp.sum(query * zrow, axis=1, keepdims=True))
+        read = (query * inv).astype(BF16)
+
+        def cotangent(t=t, query=query, inv=inv, pre=pre, low=low, scale=scale, zrow=zrow):
+            grads = cot[...]
+            lean = jnp.sum(query * grads, axis=1, keepdims=True) * inv * inv
+            dq = grads * inv - lean * zrow
+            kbuf[t, me] = (dq * jnp.where(pre > 0, 1.0, low) * scale).astype(BF16)
+            for i in range(1, docs):
+                k_copy(t, i).start()
+
+        if t == ticks - 1:
+            cotangent()
+
+        def emit(c, carry, t=t, src=src, read=read):
+            y = src[:, cols(c)].astype(F32) + dot(read, a16[:, cols(c)])
+            if t == ticks - 1:
+                y_out[0, 0, :, cols(c)] = y.astype(BF16)
+            else:
+                ybuf[t, :, cols(c)] = y.astype(BF16)
+
+                @pl.when(last)
+                def _():
+                    y_mem(t, c).start()
+
+                @pl.when(jnp.logical_not(last))
+                def _():
+                    y_whole(t, c).start()
+
+            return carry
+
+        lax.fori_loop(0, sections, emit, 0)
+        if t < ticks - 1:
+            cotangent()
+            scale_mem = scale[seg:]
+
+            def values(c, src=src, scale_mem=scale_mem):
+                h = src[pl.ds(seg, mem), cols(c)].astype(F32)
+                v = h * scale_mem * gain[:, cols(c)].astype(F32)
+                return v.astype(BF16).astype(F32)
+
+            def strength(c, total, values=values):
+                return total + jnp.sum(
+                    values(c) * rate[:, cols(c)].astype(F32), axis=1, keepdims=True
+                )
+
+            logit = lax.fori_loop(0, sections, strength, jnp.zeros((mem, 1), F32))
+            beta = 1.0 / (1.0 + jnp.exp(-logit))
+            mem_query = query[seg:]
+            mem_keys = mem_query.astype(BF16)
+            mem_read = read[seg:]
+            load_g[t + 1].wait()
+
+            def write(c, total, t=t, values=values, beta=beta, mem_keys=mem_keys,
+                      mem_read=mem_read):
+                prev = dot(mem_read, a16[:, cols(c)])
+                delta = (beta * (values(c) - prev)).astype(BF16)
+                fresh = a32[:, cols(c)] + dot(mem_keys, delta, TN)
+                a32[:, cols(c)] = fresh
+                part = fresh.astype(BF16)
+                a16[:, cols(c)] = part
+                return total + dot(g[t + 1, :, cols(c)], part, NT)
+
+            cot[...] = lax.fori_loop(0, sections, write, blank)
+            z[...] = zrow + jnp.sum(mem_query * beta, axis=0, keepdims=True)
+
+        own = src[:, cols(me, span)]
+        adt[...] += dot(kbuf[t, me], own, TN)
+        for i in range(1, docs):
+            p = peer(i)
+            for c in range(per):
+                dst = fbuf.at[t, p, :, pl.ds(c * cw, cw)]
+                remote(
+                    dst, dst, send_f.at[t, c], recv_f.at[t, p, c], (sec, p)
+                ).wait_recv()
+            remote(
+                kbuf.at[t, p], kbuf.at[t, p], send_k.at[t, i], recv_k.at[t, p], (sec, p)
+            ).wait_recv()
+            adt[...] += dot(kbuf[t, p], fbuf[t, p], TN)
+
+    ad_out[0] = (adt[...] * gain_own).T
+
+    for i in range(1, docs):
+        w_copy(i).wait_send()
+        for t in range(ticks):
+            k_copy(t, i).wait_send()
+
+    @pl.when(jnp.logical_not(first))
+    def _():
+        for t in range(ticks - 1):
+            tok_copy(t).wait_send()
+
+    def drain(c, carry):
+        for t in range(ticks - 1):
+            @pl.when(last)
+            def _():
+                y_mem(t, c).wait_send()
+
+            @pl.when(jnp.logical_not(last))
+            def _():
+                y_whole(t, c).wait_send()
+
+        owner = lax.div(c, per)
+        for t in range(ticks):
+            src = h0 if t == 0 else hbuf.at[t - 1]
+
+            @pl.when(owner != me)
+            def _():
+                forward(t, src, c, owner).wait_send()
+
+        return carry
+
+    lax.fori_loop(0, sections, drain, 0)
+
+
+def one_kernel(sections, docs, h0, tok, g, w, gain, rate, store, norm):
+    rows, width = h0.shape[2:]
+    ticks, seg, keys = g.shape[2], tok.shape[2], w.shape[2]
+    span = width // docs
+    per = sections // docs
+    anywhere = pl.BlockSpec(memory_space=pl.ANY)
+    near = pl.BlockSpec(memory_space=pltpu.VMEM)
+    dma = pltpu.SemaphoreType.DMA
+    return pl.pallas_call(
+        functools.partial(fused, sections, docs, ticks, seg),
+        out_shape=(
+            jax.ShapeDtypeStruct((1, 1, rows, width), BF16),
+            jax.ShapeDtypeStruct((1, span, keys), F32),
+        ),
+        in_specs=[anywhere] * 4 + [near, near, anywhere, near],
+        out_specs=(near, near),
+        scratch_shapes=[
+            pltpu.VMEM((rows, width), BF16),
+            pltpu.VMEM((ticks - 1, rows, width), BF16),
+            pltpu.VMEM((ticks - 1, rows, width), BF16),
+            pltpu.VMEM((ticks, rows, width), BF16),
+            pltpu.VMEM((span, keys), BF16),
+            pltpu.VMEM((width, keys), BF16),
+            pltpu.VMEM((keys, width), F32),
+            pltpu.VMEM((keys, width), BF16),
+            pltpu.VMEM((1, keys), F32),
+            pltpu.VMEM((rows, keys), F32),
+            pltpu.VMEM((ticks, docs, rows, span), BF16),
+            pltpu.VMEM((ticks, docs, rows, keys), BF16),
+            pltpu.VMEM((keys, span), F32),
+            dma((3 + ticks,)),
+            dma((docs,)), dma((docs,)),
+            dma((ticks,)), dma((ticks, sections)),
+            dma((ticks, sections)), dma((ticks, sections)),
+            dma((ticks, sections)), dma((ticks, docs, per)),
+            dma((ticks, docs)), dma((ticks, docs)),
+        ],
+        compiler_params=pltpu.CompilerParams(
+            collective_id=0, has_side_effects=True, vmem_limit_bytes=50 * 2**20
+        ),
+    )(h0, tok, g, w, gain, rate, store, norm)
+
+
 def solution(mesh):
     placed = (
         P("dp", "section", None, None),
@@ -86,8 +426,16 @@
         P("dp", "section", None, None),
         P("dp", "section", None),
     )
+    sections, docs = mesh.shape["section"], mesh.shape["dp"]
+
+    def chosen(*args):
+        width = args[0].shape[3]
+        if sections % docs == 0 and width % (128 * sections) == 0:
+            return one_kernel(sections, docs, *args)
+        return per_device(*args)
+
     return jax.shard_map(
-        per_device,
+        chosen,
         mesh=mesh,
         in_specs=placed,
         out_specs=(P("dp", "section", None, None), P("section", "dp", None)),

time: 282 us -> 132 us (0.47)
  the two profiles are of different devices: /device:TPU:0 before, /device:TPU:11 now
where the time goes in v1:
time: 132 us; the launch traced here: 131 us
  Pallas kernels  125 us (95%)
  local copies, waits for them, and re-layouts  6.05 us (5%)
    pallas_call x1, Pallas kernels, one_kernel(): pl.pallas_call(functools.partial(fused, sections, docs, ticks, seg), out_...  125 us
    unnamed x12, local copies, waits for them, and re-layouts  6.05 us

profile of v1, /device:TPU:11, one launch (start us, length us, event | category | flops | bytes accessed | tf_op | source)
XLA Modules:
  0.0 131.5 jit_solution(13757928470335673446)
XLA Ops:
  0.6 0.0 copy-start
  0.6 1.0 copy-done
  1.7 0.0 copy-start.1
  1.7 1.0 copy-done.1
  2.6 0.0 copy-start.2
  2.6 0.7 copy-done.2
  3.4 0.0 copy-start.3
  3.4 0.7 copy-done.3
  4.1 0.0 copy-start.4
  4.1 0.7 copy-done.4
  4.7 124.8 %shard_map.95 = (bf16[1,1,144,5120]{3,2,1,0:T(8,128)(2,1)S(1)}, f32[1,1280,128]{2,1,0:T(8,128)S(1)}) custom-call(bf16[1,1,144,5120]{3,2,1,0:T(8,128)(2,1)} %h0_any.1, bf16[1,3,128,640]{3,2,1,0:T(8,128)(2,1)S(1)} %copy-done, bf16[1,1,4,144,5120]{4,3,2,1,0:T(8,128)(2,1)} %g_any.1, bf16[1,1280,128]{2,1,0:T(8,128)(2,1)S(1)} %copy-done.1, ...), custom_call_target="tpu_custom_call" | custom-call | tf_op jit(solution)/shard_map/pallas_call | solution.py:383
  129.5 1.1 copy.12
  130.7 0.8 copy.13
Async XLA Ops:
  0.6 1.0 copy-start
  1.7 1.0 copy-start.1
  2.6 0.7 copy-start.2
  3.4 0.7 copy-start.3
  4.1 0.7 copy-start.4

commit v2 on v1

--- a/solution.py
+++ b/solution.py
@@ -97,6 +97,7 @@
     h0, hbuf, ybuf, g, w_own, w, a32, a16, z, cot, fbuf, kbuf, adt,
     load_sem, send_w, recv_w, send_tok, recv_tok, send_y, recv_y,
     send_f, recv_f, send_k, recv_k,
+    head_h, head_a, head_p, send_hh, recv_hh, send_ha, recv_ha, send_hp, recv_hp,
 ):
     sec, me = lax.axis_index("section"), lax.axis_index("dp")
     rows, width = h0.shape
@@ -105,6 +106,7 @@
     cw = width // sections
     per = span // cw
     follower = lax.rem(sec + 1, sections)
+    heads = head_h.shape[0]
     first, last = sec == 0, sec == sections - 1
 
     def peer(i):
@@ -171,8 +173,7 @@
 
     @pl.when(jnp.logical_not(first))
     def _():
-        for t in range(ticks - 1):
-            tok_copy(t).start()
+        tok_copy(0).start()
 
     @pl.when(first)
     def _():
@@ -205,19 +206,41 @@
             kbuf.at[t, me], kbuf.at[t, me], send_k.at[t, i], recv_k.at[t, me], (sec, peer(i))
         )
 
+    def head_copies(c):
+        to = (follower, me)
+        return (
+            remote(h0.at[:, cols(c)], head_h.at[c], send_hh.at[c], recv_hh.at[c], to),
+            remote(a16.at[:, cols(c)], head_a.at[c], send_ha.at[c], recv_ha.at[c], to),
+        )
+
+    def head_read():
+        return remote(head_p.at[0], head_p.at[1], send_hp.at[0], recv_hp.at[0], (follower, me))
+
     z[...] = z_in[0]
     load_a.wait()
+
+    def narrow(c, carry):
+        a16[:, cols(c)] = a32[:, cols(c)].astype(BF16)
+        return carry
+
+    lax.fori_loop(0, heads, narrow, 0)
+    load_h.wait()
+
+    @pl.when(jnp.logical_not(last))
+    def _():
+        for c in range(heads):
+            for copy in head_copies(c):
+                copy.start()
+
+    lax.fori_loop(heads, sections, narrow, 0)
     load_g[0].wait()
 
     def first_cot(c, total):
-        part = a32[:, cols(c)].astype(BF16)
-        a16[:, cols(c)] = part
-        return total + dot(g[0, :, cols(c)], part, NT)
+        return total + dot(g[0, :, cols(c)], a16[:, cols(c)], NT)
 
     blank = jnp.zeros((rows, keys), F32)
     cot[...] = lax.fori_loop(0, sections, first_cot, blank)
     adt[...] = jnp.zeros_like(adt)
-    load_h.wait()
     for i in range(1, docs):
         w_wait(i)
 
@@ -232,7 +255,23 @@
                     tok_wait(t - 1, c)
                     y_mem(t - 1, c).wait_recv()
 
-                @pl.when(jnp.logical_not(first))
+                whole = jnp.logical_not(first)
+                if t == 1:
+                    @pl.when(jnp.logical_and(whole, c < heads))
+                    def _():
+                        @pl.when(c == 0)
+                        def _():
+                            head_read().wait_recv()
+
+                        for copy in head_copies(lax.min(c, heads - 1)):
+                            copy.wait_recv()
+                        at = lax.min(c, heads - 1)
+                        y = head_h[at].astype(F32) + dot(head_p[1], head_a[at])
+                        hbuf[0, :, cols(c)] = y.astype(BF16)
+
+                    whole = jnp.logical_and(whole, c >= heads)
+
+                @pl.when(whole)
                 def _():
                     y_whole(t - 1, c).wait_recv()
 
@@ -268,6 +307,13 @@
             for i in range(1, docs):
                 k_copy(t, i).start()
 
+        if t == 0:
+            head_p[0] = read
+
+            @pl.when(jnp.logical_not(last))
+            def _():
+                head_read().start()
+
         if t == ticks - 1:
             cotangent()
 
@@ -282,13 +328,22 @@
                 def _():
                     y_mem(t, c).start()
 
-                @pl.when(jnp.logical_not(last))
+                whole = jnp.logical_not(last)
+                if t == 0:
+                    whole = jnp.logical_and(whole, c >= heads)
+
+                @pl.when(whole)
                 def _():
                     y_whole(t, c).start()
 
             return carry
 
         lax.fori_loop(0, sections, emit, 0)
+        if 0 < t + 1 < ticks - 1:
+            @pl.when(jnp.logical_not(first))
+            def _():
+                tok_copy(t + 1).start()
+
         if t < ticks - 1:
             cotangent()
             scale_mem = scale[seg:]
@@ -309,6 +364,13 @@
             mem_keys = mem_query.astype(BF16)
             mem_read = read[seg:]
             load_g[t + 1].wait()
+            if t == 0:
+                @pl.when(jnp.logical_not(last))
+                def _():
+                    head_read().wait_send()
+                    for c in range(heads):
+                        for copy in head_copies(c):
+                            copy.wait_send()
 
             def write(c, total, t=t, values=values, beta=beta, mem_keys=mem_keys,
                       mem_read=mem_read):
@@ -355,7 +417,11 @@
             def _():
                 y_mem(t, c).wait_send()
 
-            @pl.when(jnp.logical_not(last))
+            whole = jnp.logical_not(last)
+            if t == 0:
+                whole = jnp.logical_and(whole, c >= heads)
+
+            @pl.when(whole)
             def _():
                 y_whole(t, c).wait_send()
 
@@ -377,6 +443,7 @@
     ticks, seg, keys = g.shape[2], tok.shape[2], w.shape[2]
     span = width // docs
     per = sections // docs
+    heads = sections // 4
     anywhere = pl.BlockSpec(memory_space=pl.ANY)
     near = pl.BlockSpec(memory_space=pltpu.VMEM)
     dma = pltpu.SemaphoreType.DMA
@@ -408,9 +475,13 @@
             dma((ticks, sections)), dma((ticks, sections)),
             dma((ticks, sections)), dma((ticks, docs, per)),
             dma((ticks, docs)), dma((ticks, docs)),
+            pltpu.VMEM((heads, rows, width // sections), BF16),
+            pltpu.VMEM((heads, keys, width // sections), BF16),
+            pltpu.VMEM((2, rows, keys), BF16),
+            dma((heads,)), dma((heads,)), dma((heads,)), dma((heads,)), dma((1,)), dma((1,)),
         ],
         compiler_params=pltpu.CompilerParams(
-            collective_id=0, has_side_effects=True, vmem_limit_bytes=50 * 2**20
+            collective_id=0, has_side_effects=True, vmem_limit_bytes=63 * 2**20
         ),
     )(h0, tok, g, w, gain, rate, store, norm)
 

time: 132 us -> 125 us (0.947)
  Pallas kernels: 125 us -> 121 us
  local copies, waits for them, and re-layouts: 6.05 us -> 3.48 us
    pallas_call x1, Pallas kernels: 125 us -> 121 us  [one_kernel(): pl.pallas_call(functools.partial(fused, sections, docs, ticks, seg), out_...]
    unnamed x12 -> x4, local copies, waits for them, and re-layouts: 6.05 us -> 3.48 us
where the time goes in v2:
time: 125 us
  Pallas kernels  121 us (97%)
  local copies, waits for them, and re-layouts  3.48 us (3%)
    pallas_call x1, Pallas kernels, one_kernel(): pl.pallas_call(functools.partial(fused, sections, docs, ticks, seg), out_...  121 us
    unnamed x4, local copies, waits for them, and re-layouts  3.48 us

profile of v2, /device:TPU:11, one launch (start us, length us, event | category | flops | bytes accessed | tf_op | source)
XLA Modules:
  0.0 124.7 jit_solution(12321958970727532231)
XLA Ops:
  0.6 120.6 %shard_map.95 = (bf16[1,1,144,5120]{3,2,1,0:T(8,128)(2,1)}, f32[1,1280,128]{2,1,0:T(8,128)}) custom-call(bf16[1,1,144,5120]{3,2,1,0:T(8,128)(2,1)} %h0_any.1, bf16[1,3,128,640]{3,2,1,0:T(8,128)(2,1)} %tok_any.1, bf16[1,1,4,144,5120]{4,3,2,1,0:T(8,128)(2,1)} %g_any.1, bf16[1,1280,128]{2,1,0:T(8,128)(2,1)} %w_any.1, bf16[1,5120]{1,0:T(2,128)(2,1)} %gain.1, ...), custom_call_target="tpu_custom_call" | custom-call | tf_op jit(solution)/shard_map/pallas_call | solution.py:450
  121.2 0.0 copy-start
  121.2 2.6 %copy.12 = bf16[1,1,144,5120]{3,2,1,0:T(8,128)(2,1)} copy(bf16[1,1,144,5120]{3,2,1,0:T(8,128)(2,1)} %get-tuple-element.4) | data formatting | bytes 2949120
  123.9 0.0 copy-done
  123.9 0.8 copy.13
Async XLA Ops:
  121.2 2.7 %copy-start = (f32[1,1280,128]{2,1,0:T(8,128)S(1)}, f32[1,1280,128]{2,1,0:T(8,128)}, u32[]{:S(2)}) copy-start(f32[1,1280,128]{2,1,0:T(8,128)} %get-tuple-element.5) | copy-start | bytes 1966084

commit v3 on v2

--- a/solution.py
+++ b/solution.py
@@ -244,6 +244,22 @@
     for i in range(1, docs):
         w_wait(i)
 
+    def collect(t):
+        src = h0 if t == 0 else hbuf.at[t - 1]
+        own = src[:, cols(me, span)]
+        adt[...] += dot(kbuf[t, me], own, TN)
+        for i in range(1, docs):
+            p = peer(i)
+            for c in range(per):
+                dst = fbuf.at[t, p, :, pl.ds(c * cw, cw)]
+                remote(
+                    dst, dst, send_f.at[t, c], recv_f.at[t, p, c], (sec, p)
+                ).wait_recv()
+            remote(
+                kbuf.at[t, p], kbuf.at[t, p], send_k.at[t, i], recv_k.at[t, p], (sec, p)
+            ).wait_recv()
+            adt[...] += dot(kbuf[t, p], fbuf[t, p], TN)
+
     for t in range(ticks):
         src = h0 if t == 0 else hbuf.at[t - 1]
 
@@ -338,7 +354,7 @@
 
             return carry
 
-        lax.fori_loop(0, sections, emit, 0)
+        lax.fori_loop(0, sections, emit, 0, unroll=4 if t == ticks - 1 else 1)
         if 0 < t + 1 < ticks - 1:
             @pl.when(jnp.logical_not(first))
             def _():
@@ -385,19 +401,10 @@
             cot[...] = lax.fori_loop(0, sections, write, blank)
             z[...] = zrow + jnp.sum(mem_query * beta, axis=0, keepdims=True)
 
-        own = src[:, cols(me, span)]
-        adt[...] += dot(kbuf[t, me], own, TN)
-        for i in range(1, docs):
-            p = peer(i)
-            for c in range(per):
-                dst = fbuf.at[t, p, :, pl.ds(c * cw, cw)]
-                remote(
-                    dst, dst, send_f.at[t, c], recv_f.at[t, p, c], (sec, p)
-                ).wait_recv()
-            remote(
-                kbuf.at[t, p], kbuf.at[t, p], send_k.at[t, i], recv_k.at[t, p], (sec, p)
-            ).wait_recv()
-            adt[...] += dot(kbuf[t, p], fbuf[t, p], TN)
+        if 0 < t < ticks - 1:
+            collect(t - 1)
+        if t >= ticks - 2:
+            collect(t)
 
     ad_out[0] = (adt[...] * gain_own).T
 

time: 125 us -> 124 us (level)
  no operation moved by 1% of the time
where the time goes in v3:
time: 124 us
  Pallas kernels  120 us (97%)
  local copies, waits for them, and re-layouts  3.48 us (3%)
    pallas_call x1, Pallas kernels, one_kernel(): pl.pallas_call(functools.partial(fused, sections, docs, ticks, seg), out_...  120 us
    unnamed x4, local copies, waits for them, and re-layouts  3.48 us

profile of v3, /device:TPU:11, one launch (start us, length us, event | category | flops | bytes accessed | tf_op | source)
XLA Modules:
  0.0 123.8 jit_solution(13246459271375400398)
XLA Ops:
  0.6 119.7 %shard_map.95 = (bf16[1,1,144,5120]{3,2,1,0:T(8,128)(2,1)}, f32[1,1280,128]{2,1,0:T(8,128)}) custom-call(bf16[1,1,144,5120]{3,2,1,0:T(8,128)(2,1)} %h0_any.1, bf16[1,3,128,640]{3,2,1,0:T(8,128)(2,1)} %tok_any.1, bf16[1,1,4,144,5120]{4,3,2,1,0:T(8,128)(2,1)} %g_any.1, bf16[1,1280,128]{2,1,0:T(8,128)(2,1)} %w_any.1, bf16[1,5120]{1,0:T(2,128)(2,1)} %gain.1, ...), custom_call_target="tpu_custom_call" | custom-call | tf_op jit(solution)/shard_map/pallas_call | solution.py:457
  120.3 0.0 copy-start
  120.3 2.6 %copy.12 = bf16[1,1,144,5120]{3,2,1,0:T(8,128)(2,1)} copy(bf16[1,1,144,5120]{3,2,1,0:T(8,128)(2,1)} %get-tuple-element.4) | data formatting | bytes 2949120
  123.0 0.0 copy-done
  123.0 0.8 copy.13
Async XLA Ops:
  120.3 2.7 %copy-start = (f32[1,1280,128]{2,1,0:T(8,128)S(1)}, f32[1,1280,128]{2,1,0:T(8,128)}, u32[]{:S(2)}) copy-start(f32[1,1280,128]{2,1,0:T(8,128)} %get-tuple-element.5) | copy-start | bytes 1966084
